TPU v7x, 32 devices: a whole 2x2x4 slice. The times are simulated.
32 devices in a mesh: lon: 8 (over z, x), lat: 4 (over y, core).
Axes of the slice: x: 2, y: 2, z: 4, core: 2. Of those that a mesh axis runs over, the one named last changes fastest.
Arguments:
- fields: float32 [5, 4, 128, 1024], P(None, None, 'lat', 'lon'), may hold values from -6 to 6
- depth: int32 [128], P('lat'), may hold values from 0 to 96, as said below
- frac: float32 [4, 128, 1024], P(None, 'lat', 'lon'), may hold values from 0 to 1
- helm: float32 [4, 128, 1024], P(None, 'lat', 'lon'), may hold values from 0.1 to 2
Outputs:
- departed: float32 [5, 4, 128, 1024], P(None, None, 'lat', 'lon')
- pressure: float32 [4, 128, 1024], P(None, 'lat', 'lon')
Inputs may be any that keep to these rules, and one draw needn't show every extreme that they name: All rows of an aligned band of 8 latitude rows share one depth. A band's depth is either 96 (a jet band) or at most 32, and may be 0. Among the 32 rows of one device (aligned blocks) at most 1 band is a jet band, and in every draw some block has exactly 1.
All inputs are finite; a program needn't handle non-finite values.
Results may differ from a plain program's by a relative error of at most 0.0003.
Values sent between devices are 32-bit elements; how exact they have to be, the bound alone decides.
A program may use at most 128 MiB of HBM per device.

v0:
```python
import jax
import jax.numpy as jnp
from jax import lax
from jax.sharding import PartitionSpec as P

BAND = 8
MAXD = 96


def with_halo(cells, sides, width, closed):
    for axis, dim in sides:
        count = lax.axis_size(axis)
        ends = count if closed else count - 1
        head = lax.slice_in_dim(cells, 0, width, axis=dim)
        tail = lax.slice_in_dim(cells, cells.shape[dim] - width, cells.shape[dim], axis=dim)
        cells = jnp.concatenate(
            [
                lax.ppermute(tail, axis, [(i, (i + 1) % count) for i in range(ends)]),
                cells,
                lax.ppermute(head, axis, [((i + 1) % count, i) for i in range(ends)]),
            ],
            axis=dim,
        )
    return cells


def interp_weights(frac):
    s = -frac
    return [
        s * (s + 1.0) * (s + 2.0) / 6.0,
        -(s - 1.0) * (s + 1.0) * (s + 2.0) / 2.0,
        (s - 1.0) * s * (s + 2.0) / 2.0,
        -(s - 1.0) * s * (s + 1.0) / 6.0,
    ]


def relax(rhs, helm, lon_ext, lat_ext):
    beside_all = lon_ext[:, :, 2:] + lon_ext[:, :, :-2] + lat_ext[:, 2:, :] + lat_ext[:, :-2, :]
    return (rhs + beside_all) / (4.0 + helm)


def local(fields, depth, frac, helm):
    clon = fields.shape[3]
    lev = fields.shape[1]
    clat = fields.shape[2]
    per_block = clat // BAND
    band_depth = depth[::BAND]
    rim_width = MAXD + 2
    extended = with_halo(fields, (("lon", 3),), rim_width, True)
    extended = extended[:, :, :, : rim_width + clon + 1]
    wide = extended.shape[3]
    banded = extended.reshape(5, lev, per_block, BAND, wide)
    starts = rim_width - band_depth - 2

    def window(block, start):
        return lax.dynamic_slice_in_dim(block, start, clon + 3, axis=3)

    windows = jax.vmap(window, in_axes=(2, 0), out_axes=2)(banded, starts)
    windows = windows.reshape(5, lev, clat, clon + 3)
    weights = interp_weights(frac)
    offsets = [-1, 0, 1, 2]
    total = jnp.zeros_like(fields)
    for offset, weight in zip(offsets, weights):
        picked = windows[:, :, :, 2 - offset : 2 - offset + clon]
        total = total + weight[None] * picked
    u_wind, v_wind, phi = (total[0], total[1], total[3])
    u_ext = with_halo(u_wind, (("lon", 2),), 1, True)
    v_ext = with_halo(v_wind, (("lat", 1),), 1, False)
    div = 0.5 * (u_ext[:, :, 2:] - u_ext[:, :, :-2] + v_ext[:, 2:, :] - v_ext[:, :-2, :])
    rhs = phi - 0.5 * div
    pressure = phi
    for sweep in range(2):
        lon_ext = with_halo(pressure, (("lon", 2),), 1, True)
        lat_ext = with_halo(pressure, (("lat", 1),), 1, False)
        pressure = relax(rhs, helm, lon_ext, lat_ext)
    return (total, pressure)


def solution(mesh):
    placed = (P(None, None, "lat", "lon"), P("lat"), P(None, "lat", "lon"), P(None, "lat", "lon"))
    return jax.shard_map(
        local,
        mesh=mesh,
        in_specs=placed,
        out_specs=(P(None, None, "lat", "lon"), P(None, "lat", "lon")),
        check_vma=False,
    )
```

profile of v0, /device:TPU:30, one launch (start us, length us, event | category | flops | bytes accessed | tf_op | source)
XLA Modules:
  0.0 87.1 jit_solution(11847317696592979016)
XLA Ops:
  0.6 1.3 %fusion.29 = (f32[5,4,32,98]{3,2,1,0:T(8,128)S(1)}, f32[5,4,32,98]{3,2,1,0:T(8,128)S(1)}) fusion(f32[5,4,32,128]{3,2,1,0:T(8,128)} %param.4), kind=kLoop, calls=%fused_computation.59 | loop fusion | bytes 1003520 | tf_op jit(solution)/shard_map/slice | solution.py:15
  1.9 0.6 collective-permute-start.1
  2.5 4.2 %collective-permute-start = (f32[5,4,32,98]{3,2,1,0:T(8,128)S(1)}, f32[5,4,32,98]{3,2,1,0:T(8,128)S(1)}, u32[]{:S(2)}, u32[]{:S(2)}) collective-permute-start(f32[5,4,32,98]{3,2,1,0:T(8,128)S(1)} %get-tuple-element.7), channel_id=1, source_target_pairs={{0,4},{4,8},{8,12},{12,16},{16,20},{20,24},{24,28},{28,0},{1,5},{5... | collective-permute-start | bytes 752648 | tf_op jit(solution)/shard_map/ppermute | solution.py:18
  6.7 0.7 slice.120
  7.5 0.9 %fusion.5 = (f32[4,32,128]{2,1,0:T(8,128)S(1)}, f32[4,32,128]{2,1,0:T(8,128)S(1)}, f32[4,32,128]{2,1,0:T(8,128)S(1)}, f32[4,32,128]{2,1,0:T(8,128)S(1)}) fusion(f32[4,32,128]{2,1,0:T(8,128)} %param.6), kind=kLoop, calls=%fused_computation.19 | loop fusion | flops 278528 | bytes 327680 | tf_op jit(solution)/shard_map/div | solution.py:30
  8.3 8.2 %collective-permute-done.1 = f32[5,4,32,98]{3,2,1,0:T(8,128)S(1)} collective-permute-done((f32[5,4,32,98]{3,2,1,0:T(8,128)S(1)}, f32[5,4,32,98]{3,2,1,0:T(8,128)S(1)}, u32[]{:S(2)}, u32[]{:S(2)}) %collective-permute-start.1) | collective-permute-done | bytes 250912 | tf_op jit(solution)/shard_map/ppermute | solution.py:20
  16.5 2.2 %collective-permute-done = f32[5,4,32,98]{3,2,1,0:T(8,128)S(1)} collective-permute-done((f32[5,4,32,98]{3,2,1,0:T(8,128)S(1)}, f32[5,4,32,98]{3,2,1,0:T(8,128)S(1)}, u32[]{:S(2)}, u32[]{:S(2)}) %collective-permute-start) | collective-permute-done | bytes 250912 | tf_op jit(solution)/shard_map/ppermute | solution.py:18
  18.7 1.3 %fusion = f32[5,4,4,8,227]{4,3,2,1,0:T(8,128)S(1)} fusion(f32[5,4,32,98]{3,2,1,0:T(8,128)S(1)} %collective-permute-done.1, f32[5,4,32,128]{3,2,1,0:T(8,128)} %param.4, f32[5,4,32,98]{3,2,1,0:T(8,128)S(1)} %collective-permute-done), kind=kLoop, calls=%fused_computation.2 | loop fusion | flops 290560 | bytes 1410560 | tf_op jit(solution)/shard_map/reshape | solution.py:52
  20.0 10.4 %copy.6 = f32[5,4,4,8,227]{3,0,1,2,4:T(8,128)} copy(f32[5,4,4,8,227]{4,3,2,1,0:T(8,128)S(1)} %fusion) | data formatting | bytes 1162240 | tf_op jit(solution)/shard_map/reshape | solution.py:52
  30.4 9.7 %gather_fusion = f32[4,5,4,8,131]{3,1,2,4,0:T(8,128)} fusion(f32[4,5,4,8,227]{3,1,2,0,4:T(8,128)} %bitcast.20, s32[4]{0:T(128)S(1)} %fusion.27), kind=kCustom, calls=%fused_computation | custom fusion | bytes 670800 | tf_op jit(solution)/shard_map/vmap()/gather | solution.py:56
  40.1 5.5 %copy.7 = f32[5,4,4,8,131]{4,3,2,1,0:T(8,128)S(1)} copy(f32[5,4,4,8,131]{3,0,1,4,2:T(8,128)} %bitcast.21) | data formatting | bytes 670720 | tf_op jit(solution)/shard_map/vmap()/transpose | solution.py:58
  45.6 0.3 fusion.1
  46.0 0.1 fusion.34
  46.0 1.9 %collective-permute-start.9 = (f32[4,1,128]{2,1,0:T(1,128)S(1)}, f32[4,1,128]{2,1,0:T(1,128)S(1)}, u32[]{:S(2)}, u32[]{:S(2)}) collective-permute-start(f32[4,1,128]{2,1,0:T(1,128)S(1)} %get-tuple-element.20), channel_id=1, source_target_pairs={{0,1},{1,2},{2,3},{4,5},{5,6},{6,7},{8,9},{9,10},{10,11},{12,13},{... | collective-permute-start | bytes 6152 | tf_op jit(solution)/shard_map/ppermute | solution.py:18
  48.0 3.6 %collective-permute-start.8 = (f32[4,1,128]{2,1,0:T(1,128)S(1)}, f32[4,1,128]{2,1,0:T(1,128)S(1)}, u32[]{:S(2)}, u32[]{:S(2)}) collective-permute-start(f32[4,1,128]{2,1,0:T(1,128)S(1)} %get-tuple-element.19), channel_id=1, source_target_pairs={{1,0},{2,1},{3,2},{5,4},{6,5},{7,6},{9,8},{10,9},{11,10},{13,12},{... | collective-permute-start | bytes 6152 | tf_op jit(solution)/shard_map/ppermute | solution.py:20
  51.7 2.0 %collective-permute-start.6 = (f32[4,32,1]{2,1,0:T(8,128)S(1)}, f32[4,32,1]{2,1,0:T(8,128)S(1)}, u32[]{:S(2)}, u32[]{:S(2)}) collective-permute-start(f32[4,32,1]{2,1,0:T(8,128)S(1)} %get-tuple-element.17), channel_id=1, source_target_pairs={{4,0},{8,4},{12,8},{16,12},{20,16},{24,20},{28,24},{0,28},{5,1},{9... | collective-permute-start | bytes 1544 | tf_op jit(solution)/shard_map/ppermute | solution.py:20
  53.7 1.9 %collective-permute-start.5 = (f32[4,1,128]{2,1,0:T(1,128)S(1)}, f32[4,1,128]{2,1,0:T(1,128)S(1)}, u32[]{:S(2)}, u32[]{:S(2)}) collective-permute-start(f32[4,1,128]{2,1,0:T(1,128)S(1)} %get-tuple-element.16), channel_id=1, source_target_pairs={{0,1},{1,2},{2,3},{4,5},{5,6},{6,7},{8,9},{9,10},{10,11},{12,13},{... | collective-permute-start | bytes 6152 | tf_op jit(solution)/shard_map/ppermute | solution.py:18
  55.6 1.0 %collective-permute-done.7 = f32[4,32,1]{2,1,0:T(8,128)S(1)} collective-permute-done((f32[4,32,1]{2,1,0:T(8,128)S(1)}, f32[4,32,1]{2,1,0:T(8,128)S(1)}, u32[]{:S(2)}, u32[]{:S(2)}) %collective-permute-start.7) | collective-permute-done | bytes 544 | tf_op jit(solution)/shard_map/ppermute | solution.py:18
  56.6 2.6 %collective-permute-start.4 = (f32[4,1,128]{2,1,0:T(1,128)S(1)}, f32[4,1,128]{2,1,0:T(1,128)S(1)}, u32[]{:S(2)}, u32[]{:S(2)}) collective-permute-start(f32[4,1,128]{2,1,0:T(1,128)S(1)} %get-tuple-element.15), channel_id=1, source_target_pairs={{1,0},{2,1},{3,2},{5,4},{6,5},{7,6},{9,8},{10,9},{11,10},{13,12},{... | collective-permute-start | bytes 6152 | tf_op jit(solution)/shard_map/ppermute | solution.py:20
  59.3 0.1 fusion.32
  59.4 2.8 %collective-permute-start.3 = (f32[4,32,1]{2,1,0:T(8,128)S(1)}, f32[4,32,1]{2,1,0:T(8,128)S(1)}, u32[]{:S(2)}, u32[]{:S(2)}) collective-permute-start(f32[4,32,1]{2,1,0:T(8,128)S(1)} %get-tuple-element.14), channel_id=1, source_target_pairs={{0,4},{4,8},{8,12},{12,16},{16,20},{20,24},{24,28},{28,0},{1,5},{5... | collective-permute-start | bytes 1544 | tf_op jit(solution)/shard_map/ppermute | solution.py:18
  62.2 1.9 %collective-permute-done.3 = f32[4,32,1]{2,1,0:T(8,128)S(1)} collective-permute-done((f32[4,32,1]{2,1,0:T(8,128)S(1)}, f32[4,32,1]{2,1,0:T(8,128)S(1)}, u32[]{:S(2)}, u32[]{:S(2)}) %collective-permute-start.3) | collective-permute-done | bytes 544 | tf_op jit(solution)/shard_map/ppermute | solution.py:18
  64.1 1.7 %collective-permute-start.2 = (f32[4,32,1]{2,1,0:T(8,128)S(1)}, f32[4,32,1]{2,1,0:T(8,128)S(1)}, u32[]{:S(2)}, u32[]{:S(2)}) collective-permute-start(f32[4,32,1]{2,1,0:T(8,128)S(1)} %get-tuple-element.13), channel_id=1, source_target_pairs={{4,0},{8,4},{12,8},{16,12},{20,16},{24,20},{28,24},{0,28},{5,1},{9... | collective-permute-start | bytes 1544 | tf_op jit(solution)/shard_map/ppermute | solution.py:20
  65.8 5.6 %collective-permute-done.2 = f32[4,32,1]{2,1,0:T(8,128)S(1)} collective-permute-done((f32[4,32,1]{2,1,0:T(8,128)S(1)}, f32[4,32,1]{2,1,0:T(8,128)S(1)}, u32[]{:S(2)}, u32[]{:S(2)}) %collective-permute-start.2) | collective-permute-done | bytes 544 | tf_op jit(solution)/shard_map/ppermute | solution.py:20
  71.4 0.2 fusion.18
  71.6 1.9 %collective-permute-start.13 = (f32[4,1,128]{2,1,0:T(1,128)S(1)}, f32[4,1,128]{2,1,0:T(1,128)S(1)}, u32[]{:S(2)}, u32[]{:S(2)}) collective-permute-start(f32[4,1,128]{2,1,0:T(1,128)S(1)} %get-tuple-element.12), channel_id=1, source_target_pairs={{0,1},{1,2},{2,3},{4,5},{5,6},{6,7},{8,9},{9,10},{10,11},{12,13},{... | collective-permute-start | bytes 6152 | tf_op jit(solution)/shard_map/ppermute | solution.py:18
  73.6 3.6 %collective-permute-start.12 = (f32[4,1,128]{2,1,0:T(1,128)S(1)}, f32[4,1,128]{2,1,0:T(1,128)S(1)}, u32[]{:S(2)}, u32[]{:S(2)}) collective-permute-start(f32[4,1,128]{2,1,0:T(1,128)S(1)} %get-tuple-element.11), channel_id=1, source_target_pairs={{1,0},{2,1},{3,2},{5,4},{6,5},{7,6},{9,8},{10,9},{11,10},{13,12},{... | collective-permute-start | bytes 6152 | tf_op jit(solution)/shard_map/ppermute | solution.py:20
  77.2 0.1 fusion.30
  77.3 2.0 %collective-permute-start.11 = (f32[4,32,1]{2,1,0:T(8,128)S(1)}, f32[4,32,1]{2,1,0:T(8,128)S(1)}, u32[]{:S(2)}, u32[]{:S(2)}) collective-permute-start(f32[4,32,1]{2,1,0:T(8,128)S(1)} %get-tuple-element.10), channel_id=1, source_target_pairs={{0,4},{4,8},{8,12},{12,16},{16,20},{20,24},{24,28},{28,0},{1,5},{5... | collective-permute-start | bytes 1544 | tf_op jit(solution)/shard_map/ppermute | solution.py:18
  79.3 2.2 %collective-permute-done.11 = f32[4,32,1]{2,1,0:T(8,128)S(1)} collective-permute-done((f32[4,32,1]{2,1,0:T(8,128)S(1)}, f32[4,32,1]{2,1,0:T(8,128)S(1)}, u32[]{:S(2)}, u32[]{:S(2)}) %collective-permute-start.11) | collective-permute-done | bytes 544 | tf_op jit(solution)/shard_map/ppermute | solution.py:18
  81.6 4.7 %collective-permute-done.10 = f32[4,32,1]{2,1,0:T(8,128)S(1)} collective-permute-done((f32[4,32,1]{2,1,0:T(8,128)S(1)}, f32[4,32,1]{2,1,0:T(8,128)S(1)}, u32[]{:S(2)}, u32[]{:S(2)}) %collective-permute-start.10) | collective-permute-done | bytes 544 | tf_op jit(solution)/shard_map/ppermute | solution.py:20
  86.3 0.8 fusion.13
  (18 shorter events, 0.1 us)
Async XLA Ops:
  1.9 14.6 %collective-permute-start.1 = (f32[5,4,32,98]{3,2,1,0:T(8,128)S(1)}, f32[5,4,32,98]{3,2,1,0:T(8,128)S(1)}, u32[]{:S(2)}, u32[]{:S(2)}) collective-permute-start(f32[5,4,32,98]{3,2,1,0:T(8,128)S(1)} %get-tuple-element.8), channel_id=1, source_target_pairs={{4,0},{8,4},{12,8},{16,12},{20,16},{24,20},{28,24},{0,28},{5,1},{9... | collective-permute-start | bytes 752648 | tf_op jit(solution)/shard_map/ppermute | solution.py:20
  2.5 16.2 %collective-permute-start = (f32[5,4,32,98]{3,2,1,0:T(8,128)S(1)}, f32[5,4,32,98]{3,2,1,0:T(8,128)S(1)}, u32[]{:S(2)}, u32[]{:S(2)}) collective-permute-start(f32[5,4,32,98]{3,2,1,0:T(8,128)S(1)} %get-tuple-element.7), channel_id=1, source_target_pairs={{0,4},{4,8},{8,12},{12,16},{16,20},{20,24},{24,28},{28,0},{1,5},{5... | collective-permute-start | bytes 752648 | tf_op jit(solution)/shard_map/ppermute | solution.py:18
  20.0 51.4 %copy-start.1 = (f32[4,32,128]{2,1,0:T(8,128)S(1)}, f32[4,32,128]{2,1,0:T(8,128)}, u32[]{:S(2)}) copy-start(f32[4,32,128]{2,1,0:T(8,128)} %param.7) | copy-start | bytes 196612
  45.9 41.1 %copy-start = (f32[5,4,32,128]{3,2,1,0:T(8,128)}, f32[5,4,32,128]{3,2,1,0:T(8,128)S(1)}, u32[]{:S(2)}) copy-start(f32[5,4,32,128]{3,2,1,0:T(8,128)S(1)} %fusion.1) | copy-start | bytes 983044
  46.0 25.4 %collective-permute-start.9 = (f32[4,1,128]{2,1,0:T(1,128)S(1)}, f32[4,1,128]{2,1,0:T(1,128)S(1)}, u32[]{:S(2)}, u32[]{:S(2)}) collective-permute-start(f32[4,1,128]{2,1,0:T(1,128)S(1)} %get-tuple-element.20), channel_id=1, source_target_pairs={{0,1},{1,2},{2,3},{4,5},{5,6},{6,7},{8,9},{9,10},{10,11},{12,13},{... | collective-permute-start | bytes 6152 | tf_op jit(solution)/shard_map/ppermute | solution.py:18
  48.0 23.4 %collective-permute-start.8 = (f32[4,1,128]{2,1,0:T(1,128)S(1)}, f32[4,1,128]{2,1,0:T(1,128)S(1)}, u32[]{:S(2)}, u32[]{:S(2)}) collective-permute-start(f32[4,1,128]{2,1,0:T(1,128)S(1)} %get-tuple-element.19), channel_id=1, source_target_pairs={{1,0},{2,1},{3,2},{5,4},{6,5},{7,6},{9,8},{10,9},{11,10},{13,12},{... | collective-permute-start | bytes 6152 | tf_op jit(solution)/shard_map/ppermute | solution.py:20
  51.6 5.0 %collective-permute-start.7 = (f32[4,32,1]{2,1,0:T(8,128)S(1)}, f32[4,32,1]{2,1,0:T(8,128)S(1)}, u32[]{:S(2)}, u32[]{:S(2)}) collective-permute-start(f32[4,32,1]{2,1,0:T(8,128)S(1)} %get-tuple-element.18), channel_id=1, source_target_pairs={{0,4},{4,8},{8,12},{12,16},{16,20},{20,24},{24,28},{28,0},{1,5},{5... | collective-permute-start | bytes 1544 | tf_op jit(solution)/shard_map/ppermute | solution.py:18
  51.7 7.7 %collective-permute-start.6 = (f32[4,32,1]{2,1,0:T(8,128)S(1)}, f32[4,32,1]{2,1,0:T(8,128)S(1)}, u32[]{:S(2)}, u32[]{:S(2)}) collective-permute-start(f32[4,32,1]{2,1,0:T(8,128)S(1)} %get-tuple-element.17), channel_id=1, source_target_pairs={{4,0},{8,4},{12,8},{16,12},{20,16},{24,20},{28,24},{0,28},{5,1},{9... | collective-permute-start | bytes 1544 | tf_op jit(solution)/shard_map/ppermute | solution.py:20
  53.7 17.7 %collective-permute-start.5 = (f32[4,1,128]{2,1,0:T(1,128)S(1)}, f32[4,1,128]{2,1,0:T(1,128)S(1)}, u32[]{:S(2)}, u32[]{:S(2)}) collective-permute-start(f32[4,1,128]{2,1,0:T(1,128)S(1)} %get-tuple-element.16), channel_id=1, source_target_pairs={{0,1},{1,2},{2,3},{4,5},{5,6},{6,7},{8,9},{9,10},{10,11},{12,13},{... | collective-permute-start | bytes 6152 | tf_op jit(solution)/shard_map/ppermute | solution.py:18
  56.6 14.8 %collective-permute-start.4 = (f32[4,1,128]{2,1,0:T(1,128)S(1)}, f32[4,1,128]{2,1,0:T(1,128)S(1)}, u32[]{:S(2)}, u32[]{:S(2)}) collective-permute-start(f32[4,1,128]{2,1,0:T(1,128)S(1)} %get-tuple-element.15), channel_id=1, source_target_pairs={{1,0},{2,1},{3,2},{5,4},{6,5},{7,6},{9,8},{10,9},{11,10},{13,12},{... | collective-permute-start | bytes 6152 | tf_op jit(solution)/shard_map/ppermute | solution.py:20
  59.4 4.7 %collective-permute-start.3 = (f32[4,32,1]{2,1,0:T(8,128)S(1)}, f32[4,32,1]{2,1,0:T(8,128)S(1)}, u32[]{:S(2)}, u32[]{:S(2)}) collective-permute-start(f32[4,32,1]{2,1,0:T(8,128)S(1)} %get-tuple-element.14), channel_id=1, source_target_pairs={{0,4},{4,8},{8,12},{12,16},{16,20},{20,24},{24,28},{28,0},{1,5},{5... | collective-permute-start | bytes 1544 | tf_op jit(solution)/shard_map/ppermute | solution.py:18
  64.1 7.3 %collective-permute-start.2 = (f32[4,32,1]{2,1,0:T(8,128)S(1)}, f32[4,32,1]{2,1,0:T(8,128)S(1)}, u32[]{:S(2)}, u32[]{:S(2)}) collective-permute-start(f32[4,32,1]{2,1,0:T(8,128)S(1)} %get-tuple-element.13), channel_id=1, source_target_pairs={{4,0},{8,4},{12,8},{16,12},{20,16},{24,20},{28,24},{0,28},{5,1},{9... | collective-permute-start | bytes 1544 | tf_op jit(solution)/shard_map/ppermute | solution.py:20
  71.6 14.7 %collective-permute-start.13 = (f32[4,1,128]{2,1,0:T(1,128)S(1)}, f32[4,1,128]{2,1,0:T(1,128)S(1)}, u32[]{:S(2)}, u32[]{:S(2)}) collective-permute-start(f32[4,1,128]{2,1,0:T(1,128)S(1)} %get-tuple-element.12), channel_id=1, source_target_pairs={{0,1},{1,2},{2,3},{4,5},{5,6},{6,7},{8,9},{9,10},{10,11},{12,13},{... | collective-permute-start | bytes 6152 | tf_op jit(solution)/shard_map/ppermute | solution.py:18
  73.6 12.7 %collective-permute-start.12 = (f32[4,1,128]{2,1,0:T(1,128)S(1)}, f32[4,1,128]{2,1,0:T(1,128)S(1)}, u32[]{:S(2)}, u32[]{:S(2)}) collective-permute-start(f32[4,1,128]{2,1,0:T(1,128)S(1)} %get-tuple-element.11), channel_id=1, source_target_pairs={{1,0},{2,1},{3,2},{5,4},{6,5},{7,6},{9,8},{10,9},{11,10},{13,12},{... | collective-permute-start | bytes 6152 | tf_op jit(solution)/shard_map/ppermute | solution.py:20
  77.3 4.3 %collective-permute-start.11 = (f32[4,32,1]{2,1,0:T(8,128)S(1)}, f32[4,32,1]{2,1,0:T(8,128)S(1)}, u32[]{:S(2)}, u32[]{:S(2)}) collective-permute-start(f32[4,32,1]{2,1,0:T(8,128)S(1)} %get-tuple-element.10), channel_id=1, source_target_pairs={{0,4},{4,8},{8,12},{12,16},{16,20},{20,24},{24,28},{28,0},{1,5},{5... | collective-permute-start | bytes 1544 | tf_op jit(solution)/shard_map/ppermute | solution.py:18
  79.3 7.0 %collective-permute-start.10 = (f32[4,32,1]{2,1,0:T(8,128)S(1)}, f32[4,32,1]{2,1,0:T(8,128)S(1)}, u32[]{:S(2)}, u32[]{:S(2)}) collective-permute-start(f32[4,32,1]{2,1,0:T(8,128)S(1)} %get-tuple-element.9), channel_id=1, source_target_pairs={{4,0},{8,4},{12,8},{16,12},{20,16},{24,20},{28,24},{0,28},{5,1},{9... | collective-permute-start | bytes 1544 | tf_op jit(solution)/shard_map/ppermute | solution.py:20
where the time goes:
time: 87.5 us; the launch traced here: 87.1 us
  starting transfers between devices  29.1 us (33%)
  local copies, waits for them, and re-layouts  27.9 us (32%)
  waiting for transfers between devices  25.9 us (30%)
  other arithmetic  3.45 us (4%)
    ppermute x7, waiting for transfers between devices, with_halo(): lax.ppermute(head, axis, [((i + 1) % count, i) for i in range(ends)])  18.5 us
    ppermute x7, starting transfers between devices, with_halo(): lax.ppermute(tail, axis, [(i, (i + 1) % count) for i in range(ends)])  14.9 us
    ppermute x7, starting transfers between devices, with_halo(): lax.ppermute(head, axis, [((i + 1) % count, i) for i in range(ends)])  14.2 us
    reshape x1, local copies, waits for them, and re-layouts, local(): banded = extended.reshape(5, lev, per_block, BAND, wide)  10.4 us
    gather x1, local copies, waits for them, and re-layouts, window(): return lax.dynamic_slice_in_dim(block, start, clon + 3, axis=3)  9.69 us
    ppermute x7, waiting for transfers between devices, with_halo(): lax.ppermute(tail, axis, [(i, (i + 1) % count) for i in range(ends)])  7.37 us
    transpose x1, local copies, waits for them, and re-layouts, local(): windows = jax.vmap(window, in_axes=(2, 0), out_axes=2)(banded, starts)  5.51 us
  transfers between devices with their start and end apart: 14, of which 7 were waited for; matrix products, arithmetic and copies ran while one was open for 2% of the time, Pallas kernels for 0%

commit v1 on v0

v1 whole, which is shorter than its diff:
```python
import functools

import jax
import jax.numpy as jnp
from jax import lax
from jax.experimental import pallas as pl
from jax.experimental.pallas import tpu as pltpu
from jax.sharding import PartitionSpec as P

BAND = 8
SHALLOW = 32
LANES = 128
NEAR = SHALLOW + 4
F32 = jnp.float32
MESH = pl.DeviceIdType.MESH
HALO_FIELDS = (0, 1, 3)
SPARE = 108


def turn(x, shift):
    shift %= LANES
    return x if shift == 0 else pltpu.roll(x, shift, axis=1)


def lane_of(shape):
    return lax.broadcasted_iota(jnp.int32, shape, len(shape) - 1)


def jet_band(depth_ref, bands):
    jet = jnp.int32(0)
    for b in range(1, bands):
        jet = jnp.where(depth_ref[b * BAND] > SHALLOW, b, jet)
    return jet


def exchange(lev, clat, depth_ref, fields_hbm, frac_hbm, helm_hbm,
             main_o, edge_o, above_o, below_o, la_o, lb_o, ra_o, rb_o,
             fields, frac, helm, main, edge, top, bottom, dtop, dbottom, gtop, gbottom,
             in_sem, send_sem, recv_sem):
    bands = clat // BAND
    loads = [
        pltpu.make_async_copy(src, dst, in_sem.at[i])
        for i, (src, dst) in enumerate(((fields_hbm, fields), (frac_hbm, frac), (helm_hbm, helm)))
    ]
    for load in loads:
        load.start()
    nlon, nlat = lax.axis_size("lon"), lax.axis_size("lat")
    i, j = lax.axis_index("lon"), lax.axis_index("lat")
    east, west = lax.rem(i + 1, nlon), lax.rem(i + nlon - 1, nlon)
    south, north = lax.rem(j + 1, nlat), lax.rem(j + nlat - 1, nlat)
    peers = [{"lon": a, "lat": b} for a, b in (
        (east, j), (west, j), (i, north), (i, south),
        (east, north), (east, south), (west, north), (west, south))]
    barrier = pltpu.get_barrier_semaphore()
    for peer in peers:
        pl.semaphore_signal(barrier, inc=1, device_id=peer, device_id_type=MESH)

    def copy(n, src, dst, peer):
        return pltpu.make_async_remote_copy(
            src_ref=src, dst_ref=dst, send_sem=send_sem.at[n], recv_sem=recv_sem.at[n],
            device_id=peers[peer], device_id_type=MESH)

    copies = [
        copy(0, main, main_o, 0),
        copy(1, edge, edge_o, 1),
        copy(2, top, below_o, 2),
        copy(3, bottom, above_o, 3),
        copy(4, dtop, lb_o, 4),
        copy(5, dbottom, la_o, 5),
        copy(6, gtop, rb_o, 6),
        copy(7, gbottom, ra_o, 7),
    ]
    jet = jet_band(depth_ref, bands)
    for load in loads:
        load.wait()
    nf = 5 * lev * BAND
    lane = lane_of((nf, LANES))
    jet = jnp.full((nf, LANES), jet)
    x = [fields[:, :, pl.ds(b * BAND, BAND), :].reshape(nf, LANES) for b in range(bands)]
    whole = x[0]
    for b in range(1, bands):
        whole = jnp.where(jet == b, x[b], whole)
    main[0] = whole.reshape(5, lev, BAND, LANES)
    packed = None
    for slot in range(bands - 1):
        y = jnp.where(jet > slot, x[slot], x[slot + 1])
        y = turn(y, slot * NEAR + NEAR - LANES)
        packed = y if packed is None else jnp.where(lane >= slot * NEAR, y, packed)
    main[1] = packed.reshape(5, lev, BAND, LANES)
    nk = lev * BAND
    lane = lane_of((nk, LANES))
    rest = main[1, 0].reshape(nk, LANES)
    for b in range(bands):
        at = SPARE + 3 * b
        rows = pl.ds(b * BAND, BAND)
        fr = turn(frac[:, rows, :].reshape(nk, LANES), at - (LANES - 2))
        he = turn(helm[:, rows, :].reshape(nk, LANES), at + 2 - (LANES - 1))
        rest = jnp.where((lane >= at) & (lane < at + 2), fr, rest)
        rest = jnp.where(lane == at + 2, he, rest)
    main[1, 0] = rest.reshape(lev, BAND, LANES)
    pl.semaphore_wait(barrier, len(peers))
    copies[0].start()

    acc = jnp.zeros((nk, LANES), F32)
    for b in range(bands):
        rows = pl.ds(b * BAND, BAND)
        for n in range(7):
            src = fields[n, :, rows, :] if n < 5 else (frac if n == 5 else helm)[:, rows, :]
            at = 32 * b + (17 if n == 6 else 3 * n)
            wide = 3 if n < 5 else 7 - n
            acc = jnp.where((lane >= at) & (lane < at + wide), turn(src.reshape(nk, LANES), at), acc)
    edge[...] = acc.reshape(lev, BAND, LANES)
    copies[1].start()

    lane8 = lane_of((2 * lev, LANES))
    for row, mine, diag, thin, n, at_depth in (
            (0, top, dtop, gtop, 0, 0), (clat - 2, bottom, dbottom, gbottom, 1, clat - 1)):
        for q in range(5):
            src = fields.at[HALO_FIELDS[q]] if q < 3 else (frac if q == 3 else helm)
            for k in range(lev):
                mine[q, 2 * k:2 * k + 2, :] = src[k, row:row + 2, :]
        mine[5] = jnp.full((2 * lev, LANES), depth_ref[at_depth].astype(F32))
        copies[2 + n].start()
        u = jnp.where(lane8 < 2, turn(mine[3], 2), mine[0])
        diag[0] = jnp.where(lane8 == 2, turn(mine[4], 3), u)
        diag[1] = mine[1]
        diag[2] = mine[2]
        copies[4 + n].start()
        g = mine[0]
        for q in range(1, 5):
            at = 11 if q == 4 else 3 * q
            g = jnp.where(lane8 >= at, turn(mine[q], at), g)
        thin[...] = g
        copies[6 + n].start()
    for c in copies:
        c.wait()


def interp_weights(frac):
    s = -frac
    return [
        s * (s + 1.0) * (s + 2.0) / 6.0,
        -(s - 1.0) * (s + 1.0) * (s + 2.0) / 2.0,
        (s - 1.0) * s * (s + 2.0) / 2.0,
        -(s - 1.0) * s * (s + 1.0) / 6.0,
    ]


def depart(own, left, right, depth, weights):
    lane = lane_of(own[0].shape)
    totals = [jnp.zeros_like(own[0]) for _ in own]
    for o, w in zip((-1, 0, 1, 2), weights):
        s = depth + o
        t = lane + s
        shift = (s + LANES) & (LANES - 1)
        for n in range(len(own)):
            x = jnp.where(t <= LANES - 1, own[n], left[n])
            if o == -1:
                x = jnp.where(t == -1, right[n], x)
            totals[n] = totals[n] + w * pltpu.roll(x, shift, axis=1)
    return totals


def depart_beside(own, left, right, depth, weights):
    lane = lane_of(own[0].shape)
    totals = [jnp.zeros_like(own[0]) for _ in own]
    for o, w in zip((-1, 0, 1, 2), weights):
        s = depth + o
        t = lane + s
        shift = (s + LANES) & (LANES - 1)
        for n in range(len(own)):
            x = jnp.where(t <= LANES - 1, left[n], own[n])
            if o < 2:
                x = jnp.where((t >= 0) & (t <= 1), right[n], x)
            if o == -1:
                x = jnp.where(t == -1, own[n], x)
            totals[n] = totals[n] + w * pltpu.roll(x, shift, axis=1)
    return totals


def beside_pair(own, halo):
    lane = lane_of(own.shape)
    first, last = lane == 0, lane == LANES - 1
    return (
        (turn(jnp.where(first, halo, own), -1), turn(jnp.where(last, halo, own), 1)),
        (turn(jnp.where(first, own, halo), -1), turn(jnp.where(last, own, halo), 1)),
    )


def update(lev, clat, depth_ref, fields, frac, helm, main, edge, above, below, la, lb, ra, rb,
           departed, pressure, ext, hel, rhs_s, p1_s):
    bands = clat // BAND
    j = lax.axis_index("lat")
    inside = (j > 0, j < lax.axis_size("lat") - 1)
    jet = jet_band(depth_ref, bands)
    lane = lane_of((BAND, LANES))
    for k in range(lev):
        for b in range(bands):
            rows = pl.ds(b * BAND, BAND)
            depth = depth_ref[b * BAND]
            slot = b - (b > jet).astype(jnp.int32)
            amount = (2 * LANES - NEAR - NEAR * slot) & (LANES - 1)
            whole = b == jet
            own = [fields[f, k, rows, :] for f in range(5)]
            left = [jnp.where(whole, main[0, f, k], pltpu.roll(main[1, f, k], amount, axis=1)) for f in range(5)]
            right = [turn(edge[k], -(32 * b + 3 * f)) for f in range(5)]
            got = depart(own, left, right, depth, interp_weights(frac[k, rows, :]))
            for f in range(5):
                departed[f, k, rows, :] = got[f]
            fr = jnp.where(lane < 64, turn(edge[k], -(32 * b + 15)), turn(main[1, 0, k], 18 - 3 * b))
            he = jnp.where(lane < 64, turn(edge[k], -(32 * b + 17)), turn(main[1, 0, k], 17 - 3 * b))
            pick = lambda z: [z[f] for f in HALO_FIELDS]
            past = depart_beside(pick(own), pick(left), pick(right), depth, interp_weights(fr))
            at = pl.ds((b + 1) * BAND, BAND)
            for q, f in enumerate(HALO_FIELDS):
                ext[q, 0, k, at, :] = got[f]
                ext[q, 1, k, at, :] = past[q]
            hel[0, k, at, :] = helm[k, rows, :]
            hel[1, k, at, :] = he
    for side, (mine, diag, thin) in enumerate(((above, la, ra), (below, lb, rb))):
        depth = jnp.max(mine[5]).astype(jnp.int32)
        own = [mine[q] for q in range(3)]
        left = [diag[q] for q in range(3)]
        g = thin[...]
        right = [turn(g, -3 * q) for q in range(3)]
        fr = jnp.where(lane < 64, turn(g, -9), turn(left[0], -2))
        he = jnp.where(lane < 64, turn(g, -11), turn(left[0], -3))
        got = depart(own, left, right, depth, interp_weights(mine[3]))
        past = depart_beside(own, left, right, depth, interp_weights(fr))
        at = BAND - 2 if side == 0 else BAND + clat
        for k in range(lev):
            pair = slice(2 * k, 2 * k + 2)
            for q in range(3):
                ext[q, 0, k, at:at + 2, :] = jnp.where(inside[side], got[q], 0.0)[pair]
                ext[q, 1, k, at:at + 2, :] = jnp.where(inside[side], past[q], 0.0)[pair]
            hel[0, k, at:at + 2, :] = mine[4][pair]
            hel[1, k, at:at + 2, :] = he[pair]
    tall = clat + BAND
    row = lax.broadcasted_iota(jnp.int32, (tall, LANES), 0)
    outside = ((row == 0) & jnp.logical_not(inside[0])) | ((row == clat + 1) & jnp.logical_not(inside[1]))
    first = BAND - 1
    for k in range(lev):
        mid = pl.ds(first, tall)
        up, down = pl.ds(first - 1, tall), pl.ds(first + 1, tall)
        u_all = beside_pair(ext[0, 0, k, mid, :], ext[0, 1, k, mid, :])
        phi = [ext[2, h, k, mid, :] for h in range(2)]
        phi_all = beside_pair(*phi)
        for h in range(2):
            div = 0.5 * (u_all[h][0] - u_all[h][1] + ext[1, h, k, down, :] - ext[1, h, k, up, :])
            rhs = phi[h] - 0.5 * div
            around = phi_all[h][0] + phi_all[h][1] + ext[2, h, k, down, :] + ext[2, h, k, up, :]
            p1 = (rhs + around) / (4.0 + hel[h, k, mid, :])
            p1_s[h, k] = jnp.where(outside, 0.0, p1)
            if h == 0:
                rhs_s[k] = rhs
        mid = pl.ds(1, clat)
        east, west = beside_pair(p1_s[0, k, mid, :], p1_s[1, k, mid, :])[0]
        around = east + west + p1_s[0, k, pl.ds(2, clat), :] + p1_s[0, k, pl.ds(0, clat), :]
        pressure[k] = (rhs_s[k, mid, :] + around) / (4.0 + helm[k])


def local(fields, depth, frac, helm):
    lev, clat, clon = fields.shape[1:]
    nothing = pl.BlockSpec(memory_space=pl.ANY)
    vmem = pl.BlockSpec(memory_space=pltpu.VMEM)
    smem = pl.BlockSpec(memory_space=pltpu.SMEM)
    tiles = [(2, 5, lev, BAND, clon), (lev, BAND, clon), (6, 2 * lev, clon), (6, 2 * lev, clon),
             (3, 2 * lev, clon), (3, 2 * lev, clon), (2 * lev, clon), (2 * lev, clon)]
    halos = pl.pallas_call(
        functools.partial(exchange, lev, clat),
        out_shape=[jax.ShapeDtypeStruct(t, F32) for t in tiles],
        in_specs=[smem, nothing, nothing, nothing],
        out_specs=[nothing] * len(tiles),
        scratch_shapes=[
            pltpu.VMEM(fields.shape, F32), pltpu.VMEM(frac.shape, F32), pltpu.VMEM(helm.shape, F32),
            *[pltpu.VMEM(t, F32) for t in tiles],
            pltpu.SemaphoreType.DMA((3,)),
            pltpu.SemaphoreType.DMA((8,)),
            pltpu.SemaphoreType.DMA((8,)),
        ],
        compiler_params=pltpu.CompilerParams(collective_id=0, has_side_effects=True, vmem_limit_bytes=8 << 20),
        name="exchange",
    )(depth, fields, frac, helm)
    tall = clat + 2 * BAND
    return pl.pallas_call(
        functools.partial(update, lev, clat),
        out_shape=[jax.ShapeDtypeStruct(fields.shape, F32), jax.ShapeDtypeStruct(frac.shape, F32)],
        in_specs=[smem] + [vmem] * (3 + len(tiles)),
        out_specs=[vmem, vmem],
        scratch_shapes=[
            pltpu.VMEM((3, 2, lev, tall, clon), F32),
            pltpu.VMEM((2, lev, tall, clon), F32),
            pltpu.VMEM((lev, clat + BAND, clon), F32),
            pltpu.VMEM((2, lev, clat + BAND, clon), F32),
        ],
        compiler_params=pltpu.CompilerParams(vmem_limit_bytes=8 << 20),
        name="update",
    )(depth, fields, frac, helm, *halos)


def solution(mesh):
    placed = (P(None, None, "lat", "lon"), P("lat"), P(None, "lat", "lon"), P(None, "lat", "lon"))
    return jax.shard_map(
        local,
        mesh=mesh,
        in_specs=placed,
        out_specs=(P(None, None, "lat", "lon"), P(None, "lat", "lon")),
        check_vma=False,
    )
```

time: 87.5 us -> 21.2 us (0.24)
  the two profiles are of different devices: /device:TPU:30 before, /device:TPU:0 now
where the time goes in v1:
time: 21.2 us; the launch traced here: 21 us
  Pallas kernels  17 us (80%)
  local copies, waits for them, and re-layouts  3.3 us (16%)
  between operations  0.65 us (3%)
    pallas_call x1, Pallas kernels, local(): pl.pallas_call(functools.partial(exchange, lev, clat), out_shape=[jax.Sha...  13.2 us
    pallas_call x1, Pallas kernels, local(): pl.pallas_call(functools.partial(update, lev, clat), out_shape=[jax.Shape...  3.81 us
    unnamed x8, local copies, waits for them, and re-layouts  3.3 us

profile of v1, /device:TPU:0, one launch (start us, length us, event | category | flops | bytes accessed | tf_op | source)
XLA Modules:
  0.0 21.0 jit_solution(6528444635456028230)
XLA Ops:
  0.6 0.0 copy-start
  0.6 1.0 %copy-done = f32[5,4,32,128]{3,2,1,0:T(8,128)S(1)} copy-done((f32[5,4,32,128]{3,2,1,0:T(8,128)S(1)}, f32[5,4,32,128]{3,2,1,0:T(8,128)}, u32[]{:S(2)}) %copy-start) | copy-done | bytes 327704
  1.6 0.0 copy-start.1
  1.6 0.8 %copy-done.1 = f32[4,32,128]{2,1,0:T(8,128)S(1)} copy-done((f32[4,32,128]{2,1,0:T(8,128)S(1)}, f32[4,32,128]{2,1,0:T(8,128)}, u32[]{:S(2)}) %copy-start.1) | copy-done | bytes 65560
  2.4 0.0 copy-start.2
  2.4 0.8 %copy-done.2 = f32[4,32,128]{2,1,0:T(8,128)S(1)} copy-done((f32[4,32,128]{2,1,0:T(8,128)S(1)}, f32[4,32,128]{2,1,0:T(8,128)}, u32[]{:S(2)}) %copy-start.2) | copy-done | bytes 65560
  3.3 0.0 copy-start.3
  3.3 0.7 %copy-done.3 = s32[32]{0:T(128)S(1)} copy-done((s32[32]{0:T(128)S(1)}, s32[32]{0:T(128)}, u32[]{:S(2)}) %copy-start.3) | copy-done | bytes 152
  3.9 13.2 %exchange.1 = (f32[2,5,4,8,128]{4,3,2,1,0:T(8,128)S(1)}, f32[4,8,128]{2,1,0:T(8,128)S(1)}, f32[6,8,128]{2,1,0:T(8,128)S(1)}, f32[6,8,128]{2,1,0:T(8,128)S(1)}, f...) custom-call(s32[32]{0:T(128)S(1)} %copy-done.3, ...), custom_call_target="tpu_custom_call" | custom-call | tf_op jit(solution)/shard_map/exchange/pallas_call | solution.py:269
  17.2 3.8 %update.1 = (f32[5,4,32,128]{3,2,1,0:T(8,128)}, f32[4,32,128]{2,1,0:T(8,128)}) custom-call(s32[32]{0:T(128)S(1)} %copy-done.3, f32[5,4,32,128]{3,2,1,0:T(8,128)S(1)} %copy-done, f32[4,32,128]{2,1,0:T(8,128)S(1)} %copy-done.1, f32[4,32,128]{2,1,0:T(8,128)S(1)} %copy-done.2, f32[2,5,4,8,128]{4,3,2,1,0:T(8,128)S(1)} %get-tuple-element.10.main, ...), custom_call_target="tpu_custom_call" | custom-call | tf_op jit(solution)/shard_map/update/pallas_call | solution.py:285
Async XLA Ops:
  0.6 1.0 %copy-start = (f32[5,4,32,128]{3,2,1,0:T(8,128)S(1)}, f32[5,4,32,128]{3,2,1,0:T(8,128)}, u32[]{:S(2)}) copy-start(f32[5,4,32,128]{3,2,1,0:T(8,128)} %fields.1) | copy-start | bytes 983044
  1.6 0.8 %copy-start.1 = (f32[4,32,128]{2,1,0:T(8,128)S(1)}, f32[4,32,128]{2,1,0:T(8,128)}, u32[]{:S(2)}) copy-start(f32[4,32,128]{2,1,0:T(8,128)} %frac.1) | copy-start | bytes 196612
  2.4 0.8 %copy-start.2 = (f32[4,32,128]{2,1,0:T(8,128)S(1)}, f32[4,32,128]{2,1,0:T(8,128)}, u32[]{:S(2)}) copy-start(f32[4,32,128]{2,1,0:T(8,128)} %helm.1) | copy-start | bytes 196612
  3.3 0.7 %copy-start.3 = (s32[32]{0:T(128)S(1)}, s32[32]{0:T(128)}, u32[]{:S(2)}) copy-start(s32[32]{0:T(128)} %depth_ref.3) | copy-start | bytes 388

commit v2 on v1

--- a/solution.py
+++ b/solution.py
@@ -33,14 +33,15 @@
     return jet
 
 
-def exchange(lev, clat, depth_ref, fields_hbm, frac_hbm, helm_hbm,
+def exchange(lev, clat, depth_hbm, fields_hbm, frac_hbm, helm_hbm,
              main_o, edge_o, above_o, below_o, la_o, lb_o, ra_o, rb_o,
-             fields, frac, helm, main, edge, top, bottom, dtop, dbottom, gtop, gbottom,
+             depth_ref, fields, frac, helm, main, edge, top, bottom, dtop, dbottom, gtop, gbottom,
              in_sem, send_sem, recv_sem):
     bands = clat // BAND
     loads = [
         pltpu.make_async_copy(src, dst, in_sem.at[i])
-        for i, (src, dst) in enumerate(((fields_hbm, fields), (frac_hbm, frac), (helm_hbm, helm)))
+        for i, (src, dst) in enumerate(
+            ((depth_hbm, depth_ref), (fields_hbm, fields), (frac_hbm, frac), (helm_hbm, helm)))
     ]
     for load in loads:
         load.start()
@@ -70,9 +71,9 @@
         copy(6, gtop, rb_o, 6),
         copy(7, gbottom, ra_o, 7),
     ]
-    jet = jet_band(depth_ref, bands)
     for load in loads:
         load.wait()
+    jet = jet_band(depth_ref, bands)
     nf = 5 * lev * BAND
     lane = lane_of((nf, LANES))
     jet = jnp.full((nf, LANES), jet)
@@ -187,9 +188,17 @@
     )
 
 
-def update(lev, clat, depth_ref, fields, frac, helm, main, edge, above, below, la, lb, ra, rb,
-           departed, pressure, ext, hel, rhs_s, p1_s):
+def update(lev, clat, *refs):
+    sources, (departed_o, pressure_o), (ext, hel, rhs_s, p1_s), here, (departed, pressure), (in_sem, out_sem) = (
+        refs[:12], refs[12:14], refs[14:18], refs[18:30], refs[30:32], refs[32:])
+    loads = [pltpu.make_async_copy(src, dst, in_sem.at[n]) for n, (src, dst) in enumerate(zip(sources, here))]
+    for load in loads:
+        load.start()
+    depth_ref, fields, frac, helm, main, edge, above, below, la, lb, ra, rb = here
     bands = clat // BAND
+    for load in loads:
+        load.wait()
+    stores = []
     j = lax.axis_index("lat")
     inside = (j > 0, j < lax.axis_size("lat") - 1)
     jet = jet_band(depth_ref, bands)
@@ -217,6 +226,8 @@
                 ext[q, 1, k, at, :] = past[q]
             hel[0, k, at, :] = helm[k, rows, :]
             hel[1, k, at, :] = he
+        stores.append(pltpu.make_async_copy(departed.at[:, k], departed_o.at[:, k], out_sem.at[k]))
+        stores[-1].start()
     for side, (mine, diag, thin) in enumerate(((above, la, ra), (below, lb, rb))):
         depth = jnp.max(mine[5]).astype(jnp.int32)
         own = [mine[q] for q in range(3)]
@@ -257,43 +268,50 @@
         east, west = beside_pair(p1_s[0, k, mid, :], p1_s[1, k, mid, :])[0]
         around = east + west + p1_s[0, k, pl.ds(2, clat), :] + p1_s[0, k, pl.ds(0, clat), :]
         pressure[k] = (rhs_s[k, mid, :] + around) / (4.0 + helm[k])
+    stores.append(pltpu.make_async_copy(pressure, pressure_o, out_sem.at[lev]))
+    stores[-1].start()
+    for store in stores:
+        store.wait()
 
 
 def local(fields, depth, frac, helm):
     lev, clat, clon = fields.shape[1:]
-    nothing = pl.BlockSpec(memory_space=pl.ANY)
-    vmem = pl.BlockSpec(memory_space=pltpu.VMEM)
-    smem = pl.BlockSpec(memory_space=pltpu.SMEM)
+    hbm = pl.BlockSpec(memory_space=pltpu.HBM)
     tiles = [(2, 5, lev, BAND, clon), (lev, BAND, clon), (6, 2 * lev, clon), (6, 2 * lev, clon),
              (3, 2 * lev, clon), (3, 2 * lev, clon), (2 * lev, clon), (2 * lev, clon)]
     halos = pl.pallas_call(
         functools.partial(exchange, lev, clat),
         out_shape=[jax.ShapeDtypeStruct(t, F32) for t in tiles],
-        in_specs=[smem, nothing, nothing, nothing],
-        out_specs=[nothing] * len(tiles),
+        in_specs=[hbm] * 4,
+        out_specs=[hbm] * len(tiles),
         scratch_shapes=[
+            pltpu.SMEM(depth.shape, jnp.int32),
             pltpu.VMEM(fields.shape, F32), pltpu.VMEM(frac.shape, F32), pltpu.VMEM(helm.shape, F32),
             *[pltpu.VMEM(t, F32) for t in tiles],
-            pltpu.SemaphoreType.DMA((3,)),
+            pltpu.SemaphoreType.DMA((4,)),
             pltpu.SemaphoreType.DMA((8,)),
             pltpu.SemaphoreType.DMA((8,)),
         ],
-        compiler_params=pltpu.CompilerParams(collective_id=0, has_side_effects=True, vmem_limit_bytes=8 << 20),
+        compiler_params=pltpu.CompilerParams(collective_id=0, has_side_effects=True, vmem_limit_bytes=60 << 20),
         name="exchange",
     )(depth, fields, frac, helm)
     tall = clat + 2 * BAND
     return pl.pallas_call(
         functools.partial(update, lev, clat),
         out_shape=[jax.ShapeDtypeStruct(fields.shape, F32), jax.ShapeDtypeStruct(frac.shape, F32)],
-        in_specs=[smem] + [vmem] * (3 + len(tiles)),
-        out_specs=[vmem, vmem],
+        in_specs=[hbm] * (4 + len(tiles)),
+        out_specs=[hbm, hbm],
         scratch_shapes=[
             pltpu.VMEM((3, 2, lev, tall, clon), F32),
             pltpu.VMEM((2, lev, tall, clon), F32),
             pltpu.VMEM((lev, clat + BAND, clon), F32),
             pltpu.VMEM((2, lev, clat + BAND, clon), F32),
+            pltpu.SMEM(depth.shape, jnp.int32),
+            *[pltpu.VMEM(t, F32) for t in (fields.shape, frac.shape, helm.shape, *tiles, fields.shape, frac.shape)],
+            pltpu.SemaphoreType.DMA((4 + len(tiles),)),
+            pltpu.SemaphoreType.DMA((lev + 1,)),
         ],
-        compiler_params=pltpu.CompilerParams(vmem_limit_bytes=8 << 20),
+        compiler_params=pltpu.CompilerParams(vmem_limit_bytes=60 << 20),
         name="update",
     )(depth, fields, frac, helm, *halos)
 

time: 21.2 us -> 17.8 us (0.84)
  local copies, waits for them, and re-layouts: 3.3 us -> 0 us
    unnamed x8 -> x0, local copies, waits for them, and re-layouts: 3.3 us -> none
    pallas_call x1, Pallas kernels: 13.2 us -> 12.5 us  [local(): pl.pallas_call(functools.partial(exchange, lev, clat), out_shape=[jax.Sha...]
    pallas_call x1, Pallas kernels: 3.81 us -> 4.47 us  [local(): pl.pallas_call(functools.partial(update, lev, clat), out_shape=[jax.Shape...]
where the time goes in v2:
time: 17.8 us; the launch traced here: 17.6 us
  Pallas kernels  17 us (96%)
  between operations  0.64 us (4%)
    pallas_call x1, Pallas kernels, local(): pl.pallas_call(functools.partial(exchange, lev, clat), out_shape=[jax.Sha...  12.5 us
    pallas_call x1, Pallas kernels, local(): pl.pallas_call(functools.partial(update, lev, clat), out_shape=[jax.Shape...  4.47 us

profile of v2, /device:TPU:0, one launch (start us, length us, event | category | flops | bytes accessed | tf_op | source)
XLA Modules:
  0.0 17.6 jit_solution(13621477009494719515)
XLA Ops:
  0.6 12.5 %exchange.1 = (f32[2,5,4,8,128]{4,3,2,1,0:T(8,128)}, f32[4,8,128]{2,1,0:T(8,128)}, f32[6,8,128]{2,1,0:T(8,128)}, f32[6,8,128]{2,1,0:T(8,128)}, f32[3,8,128]{2,1,...) custom-call(s32[32]{0:T(128)} %refs_0_.1, f32[5,4,32,128]{3,2,1,0:T(8,128)} %refs_1_.1, ...), custom_call_target="tpu_custom_call" | custom-call | tf_op jit(solution)/shard_map/exchange/pallas_call | solution.py:282
  13.1 4.5 %update.1 = (f32[5,4,32,128]{3,2,1,0:T(8,128)}, f32[4,32,128]{2,1,0:T(8,128)}) custom-call(s32[32]{0:T(128)} %refs_0_.1, f32[5,4,32,128]{3,2,1,0:T(8,128)} %refs_1_.1, f32[4,32,128]{2,1,0:T(8,128)} %refs_2_.1, f32[4,32,128]{2,1,0:T(8,128)} %refs_3_.1, f32[2,5,4,8,128]{4,3,2,1,0:T(8,128)} %get-tuple-element.10.refs_4_, ...), custom_call_target="tpu_custom_call" | custom-call | tf_op jit(solution)/shard_map/update/pallas_call | solution.py:299

commit v3 on v2

--- a/solution.py
+++ b/solution.py
@@ -62,7 +62,7 @@
             device_id=peers[peer], device_id_type=MESH)
 
     copies = [
-        copy(0, main, main_o, 0),
+        copy(0, main.at[0], main_o.at[0], 0),
         copy(1, edge, edge_o, 1),
         copy(2, top, below_o, 2),
         copy(3, bottom, above_o, 3),
@@ -70,6 +70,7 @@
         copy(5, dbottom, la_o, 5),
         copy(6, gtop, rb_o, 6),
         copy(7, gbottom, ra_o, 7),
+        copy(8, main.at[1], main_o.at[1], 0),
     ]
     for load in loads:
         load.wait()
@@ -82,6 +83,8 @@
     for b in range(1, bands):
         whole = jnp.where(jet == b, x[b], whole)
     main[0] = whole.reshape(5, lev, BAND, LANES)
+    pl.semaphore_wait(barrier, len(peers))
+    copies[0].start()
     packed = None
     for slot in range(bands - 1):
         y = jnp.where(jet > slot, x[slot], x[slot + 1])
@@ -99,8 +102,7 @@
         rest = jnp.where((lane >= at) & (lane < at + 2), fr, rest)
         rest = jnp.where(lane == at + 2, he, rest)
     main[1, 0] = rest.reshape(lev, BAND, LANES)
-    pl.semaphore_wait(barrier, len(peers))
-    copies[0].start()
+    copies[8].start()
 
     acc = jnp.zeros((nk, LANES), F32)
     for b in range(bands):
@@ -139,11 +141,12 @@
 
 def interp_weights(frac):
     s = -frac
+    below, above = (s - 1.0) * s, (s + 1.0) * (s + 2.0)
     return [
-        s * (s + 1.0) * (s + 2.0) / 6.0,
-        -(s - 1.0) * (s + 1.0) * (s + 2.0) / 2.0,
-        (s - 1.0) * s * (s + 2.0) / 2.0,
-        -(s - 1.0) * s * (s + 1.0) / 6.0,
+        s * above * (1.0 / 6.0),
+        (s - 1.0) * above * -0.5,
+        below * (s + 2.0) * 0.5,
+        below * (s + 1.0) * (-1.0 / 6.0),
     ]
 
 
@@ -189,13 +192,17 @@
 
 
 def update(lev, clat, *refs):
-    sources, (departed_o, pressure_o), (ext, hel, rhs_s, p1_s), here, (departed, pressure), (in_sem, out_sem) = (
-        refs[:12], refs[12:14], refs[14:18], refs[18:30], refs[30:32], refs[32:])
+    sources, (departed_o, pressure_o), (ext, hel, rhs_s, p1_s, wts), here, (departed, pressure), (in_sem, out_sem) = (
+        refs[:12], refs[12:14], refs[14:19], refs[19:31], refs[31:33], refs[33:])
     loads = [pltpu.make_async_copy(src, dst, in_sem.at[n]) for n, (src, dst) in enumerate(zip(sources, here))]
-    for load in loads:
-        load.start()
+    for n in (2, 0, 1, *range(3, len(loads))):
+        loads[n].start()
     depth_ref, fields, frac, helm, main, edge, above, below, la, lb, ra, rb = here
     bands = clat // BAND
+    loads.pop(2).wait()
+    for k in range(lev):
+        for o, w in enumerate(interp_weights(frac[k])):
+            wts[o, k] = w
     for load in loads:
         load.wait()
     stores = []
@@ -213,7 +220,7 @@
             own = [fields[f, k, rows, :] for f in range(5)]
             left = [jnp.where(whole, main[0, f, k], pltpu.roll(main[1, f, k], amount, axis=1)) for f in range(5)]
             right = [turn(edge[k], -(32 * b + 3 * f)) for f in range(5)]
-            got = depart(own, left, right, depth, interp_weights(frac[k, rows, :]))
+            got = depart(own, left, right, depth, [wts[o, k, rows, :] for o in range(4)])
             for f in range(5):
                 departed[f, k, rows, :] = got[f]
             fr = jnp.where(lane < 64, turn(edge[k], -(32 * b + 15)), turn(main[1, 0, k], 18 - 3 * b))
@@ -268,8 +275,8 @@
         east, west = beside_pair(p1_s[0, k, mid, :], p1_s[1, k, mid, :])[0]
         around = east + west + p1_s[0, k, pl.ds(2, clat), :] + p1_s[0, k, pl.ds(0, clat), :]
         pressure[k] = (rhs_s[k, mid, :] + around) / (4.0 + helm[k])
-    stores.append(pltpu.make_async_copy(pressure, pressure_o, out_sem.at[lev]))
-    stores[-1].start()
+        stores.append(pltpu.make_async_copy(pressure.at[k], pressure_o.at[k], out_sem.at[lev + k]))
+        stores[-1].start()
     for store in stores:
         store.wait()
 
@@ -289,8 +296,8 @@
             pltpu.VMEM(fields.shape, F32), pltpu.VMEM(frac.shape, F32), pltpu.VMEM(helm.shape, F32),
             *[pltpu.VMEM(t, F32) for t in tiles],
             pltpu.SemaphoreType.DMA((4,)),
-            pltpu.SemaphoreType.DMA((8,)),
-            pltpu.SemaphoreType.DMA((8,)),
+            pltpu.SemaphoreType.DMA((9,)),
+            pltpu.SemaphoreType.DMA((9,)),
         ],
         compiler_params=pltpu.CompilerParams(collective_id=0, has_side_effects=True, vmem_limit_bytes=60 << 20),
         name="exchange",
@@ -306,10 +313,11 @@
             pltpu.VMEM((2, lev, tall, clon), F32),
             pltpu.VMEM((lev, clat + BAND, clon), F32),
             pltpu.VMEM((2, lev, clat + BAND, clon), F32),
+            pltpu.VMEM((4, *frac.shape), F32),
             pltpu.SMEM(depth.shape, jnp.int32),
             *[pltpu.VMEM(t, F32) for t in (fields.shape, frac.shape, helm.shape, *tiles, fields.shape, frac.shape)],
             pltpu.SemaphoreType.DMA((4 + len(tiles),)),
-            pltpu.SemaphoreType.DMA((lev + 1,)),
+            pltpu.SemaphoreType.DMA((2 * lev,)),
         ],
         compiler_params=pltpu.CompilerParams(vmem_limit_bytes=60 << 20),
         name="update",

time: 17.8 us -> 17.9 us (level)
  no operation moved by 1% of the time
where the time goes in v3:
time: 17.9 us; the launch traced here: 17.7 us
  Pallas kernels  17.1 us (96%)
  between operations  0.64 us (4%)
    pallas_call x1, Pallas kernels, local(): pl.pallas_call(functools.partial(exchange, lev, clat), out_shape=[jax.Sha...  12.6 us
    pallas_call x1, Pallas kernels, local(): pl.pallas_call(functools.partial(update, lev, clat), out_shape=[jax.Shape...  4.48 us

profile of v3, /device:TPU:0, one launch (start us, length us, event | category | flops | bytes accessed | tf_op | source)
XLA Modules:
  0.0 17.7 jit_solution(5015612752413220376)
XLA Ops:
  0.6 12.6 %exchange.1 = (f32[2,5,4,8,128]{4,3,2,1,0:T(8,128)}, f32[4,8,128]{2,1,0:T(8,128)}, f32[6,8,128]{2,1,0:T(8,128)}, f32[6,8,128]{2,1,0:T(8,128)}, f32[3,8,128]{2,1,...) custom-call(s32[32]{0:T(128)} %refs_0_.1, f32[5,4,32,128]{3,2,1,0:T(8,128)} %refs_1_.1, ...), custom_call_target="tpu_custom_call" | custom-call | tf_op jit(solution)/shard_map/exchange/pallas_call | solution.py:289
  13.2 4.5 %update.1 = (f32[5,4,32,128]{3,2,1,0:T(8,128)}, f32[4,32,128]{2,1,0:T(8,128)}) custom-call(s32[32]{0:T(128)} %refs_0_.1, f32[5,4,32,128]{3,2,1,0:T(8,128)} %refs_1_.1, f32[4,32,128]{2,1,0:T(8,128)} %refs_2_.1, f32[4,32,128]{2,1,0:T(8,128)} %refs_3_.1, f32[2,5,4,8,128]{4,3,2,1,0:T(8,128)} %get-tuple-element.10.refs_4_, ...), custom_call_target="tpu_custom_call" | custom-call | tf_op jit(solution)/shard_map/update/pallas_call | solution.py:306

commit v4 on v3

--- a/solution.py
+++ b/solution.py
@@ -209,32 +209,37 @@
     j = lax.axis_index("lat")
     inside = (j > 0, j < lax.axis_size("lat") - 1)
     jet = jet_band(depth_ref, bands)
+    nk = lev * BAND
+    lane = lane_of((nk, LANES))
+    flat = lambda x: x.reshape(nk, LANES)
+    deep = lambda x: x.reshape(lev, BAND, LANES)
+    pick = lambda z: [z[f] for f in HALO_FIELDS]
+    for b in range(bands):
+        rows = pl.ds(b * BAND, BAND)
+        depth = depth_ref[b * BAND]
+        slot = b - (b > jet).astype(jnp.int32)
+        amount = (2 * LANES - NEAR - NEAR * slot) & (LANES - 1)
+        whole = b == jet
+        own = [flat(fields[f, :, rows, :]) for f in range(5)]
+        left = [jnp.where(whole, flat(main[0, f]), pltpu.roll(flat(main[1, f]), amount, axis=1)) for f in range(5)]
+        brim = flat(edge[...])
+        right = [turn(brim, -(32 * b + 3 * f)) for f in range(5)]
+        got = depart(own, left, right, depth, [flat(wts[o, :, rows, :]) for o in range(4)])
+        rest = flat(main[1, 0])
+        fr = jnp.where(lane < 64, turn(brim, -(32 * b + 15)), turn(rest, 18 - 3 * b))
+        he = jnp.where(lane < 64, turn(brim, -(32 * b + 17)), turn(rest, 17 - 3 * b))
+        past = depart_beside(pick(own), pick(left), pick(right), depth, interp_weights(fr))
+        at = pl.ds((b + 1) * BAND, BAND)
+        for f in range(5):
+            departed[f, :, rows, :] = deep(got[f])
+        for q, f in enumerate(HALO_FIELDS):
+            ext[q, 0, :, at, :] = deep(got[f])
+            ext[q, 1, :, at, :] = deep(past[q])
+        hel[0, :, at, :] = helm[:, rows, :]
+        hel[1, :, at, :] = deep(he)
+        stores.append(pltpu.make_async_copy(departed.at[:, :, rows, :], departed_o.at[:, :, rows, :], out_sem.at[b]))
+        stores[-1].start()
     lane = lane_of((BAND, LANES))
-    for k in range(lev):
-        for b in range(bands):
-            rows = pl.ds(b * BAND, BAND)
-            depth = depth_ref[b * BAND]
-            slot = b - (b > jet).astype(jnp.int32)
-            amount = (2 * LANES - NEAR - NEAR * slot) & (LANES - 1)
-            whole = b == jet
-            own = [fields[f, k, rows, :] for f in range(5)]
-            left = [jnp.where(whole, main[0, f, k], pltpu.roll(main[1, f, k], amount, axis=1)) for f in range(5)]
-            right = [turn(edge[k], -(32 * b + 3 * f)) for f in range(5)]
-            got = depart(own, left, right, depth, [wts[o, k, rows, :] for o in range(4)])
-            for f in range(5):
-                departed[f, k, rows, :] = got[f]
-            fr = jnp.where(lane < 64, turn(edge[k], -(32 * b + 15)), turn(main[1, 0, k], 18 - 3 * b))
-            he = jnp.where(lane < 64, turn(edge[k], -(32 * b + 17)), turn(main[1, 0, k], 17 - 3 * b))
-            pick = lambda z: [z[f] for f in HALO_FIELDS]
-            past = depart_beside(pick(own), pick(left), pick(right), depth, interp_weights(fr))
-            at = pl.ds((b + 1) * BAND, BAND)
-            for q, f in enumerate(HALO_FIELDS):
-                ext[q, 0, k, at, :] = got[f]
-                ext[q, 1, k, at, :] = past[q]
-            hel[0, k, at, :] = helm[k, rows, :]
-            hel[1, k, at, :] = he
-        stores.append(pltpu.make_async_copy(departed.at[:, k], departed_o.at[:, k], out_sem.at[k]))
-        stores[-1].start()
     for side, (mine, diag, thin) in enumerate(((above, la, ra), (below, lb, rb))):
         depth = jnp.max(mine[5]).astype(jnp.int32)
         own = [mine[q] for q in range(3)]
@@ -254,29 +259,28 @@
             hel[0, k, at:at + 2, :] = mine[4][pair]
             hel[1, k, at:at + 2, :] = he[pair]
     tall = clat + BAND
-    row = lax.broadcasted_iota(jnp.int32, (tall, LANES), 0)
+    row = lax.broadcasted_iota(jnp.int32, (lev, tall, LANES), 1)
     outside = ((row == 0) & jnp.logical_not(inside[0])) | ((row == clat + 1) & jnp.logical_not(inside[1]))
     first = BAND - 1
-    for k in range(lev):
-        mid = pl.ds(first, tall)
-        up, down = pl.ds(first - 1, tall), pl.ds(first + 1, tall)
-        u_all = beside_pair(ext[0, 0, k, mid, :], ext[0, 1, k, mid, :])
-        phi = [ext[2, h, k, mid, :] for h in range(2)]
-        phi_all = beside_pair(*phi)
-        for h in range(2):
-            div = 0.5 * (u_all[h][0] - u_all[h][1] + ext[1, h, k, down, :] - ext[1, h, k, up, :])
-            rhs = phi[h] - 0.5 * div
-            around = phi_all[h][0] + phi_all[h][1] + ext[2, h, k, down, :] + ext[2, h, k, up, :]
-            p1 = (rhs + around) / (4.0 + hel[h, k, mid, :])
-            p1_s[h, k] = jnp.where(outside, 0.0, p1)
-            if h == 0:
-                rhs_s[k] = rhs
-        mid = pl.ds(1, clat)
-        east, west = beside_pair(p1_s[0, k, mid, :], p1_s[1, k, mid, :])[0]
-        around = east + west + p1_s[0, k, pl.ds(2, clat), :] + p1_s[0, k, pl.ds(0, clat), :]
-        pressure[k] = (rhs_s[k, mid, :] + around) / (4.0 + helm[k])
-        stores.append(pltpu.make_async_copy(pressure.at[k], pressure_o.at[k], out_sem.at[lev + k]))
-        stores[-1].start()
+    flat = lambda x: x.reshape(-1, LANES)
+    mid, up, down = pl.ds(first, tall), pl.ds(first - 1, tall), pl.ds(first + 1, tall)
+    u_all = beside_pair(flat(ext[0, 0, :, mid, :]), flat(ext[0, 1, :, mid, :]))
+    phi = [flat(ext[2, h, :, mid, :]) for h in range(2)]
+    phi_all = beside_pair(*phi)
+    for h in range(2):
+        div = 0.5 * (u_all[h][0] - u_all[h][1] + flat(ext[1, h, :, down, :]) - flat(ext[1, h, :, up, :]))
+        rhs = phi[h] - 0.5 * div
+        around = phi_all[h][0] + phi_all[h][1] + flat(ext[2, h, :, down, :]) + flat(ext[2, h, :, up, :])
+        p1 = (rhs + around) / (4.0 + flat(hel[h, :, mid, :]))
+        p1_s[h] = jnp.where(outside, 0.0, p1.reshape(lev, tall, LANES))
+        if h == 0:
+            rhs_s[...] = rhs.reshape(lev, tall, LANES)
+    mid = pl.ds(1, clat)
+    east, west = beside_pair(flat(p1_s[0, :, mid, :]), flat(p1_s[1, :, mid, :]))[0]
+    around = east + west + flat(p1_s[0, :, pl.ds(2, clat), :]) + flat(p1_s[0, :, pl.ds(0, clat), :])
+    pressure[...] = ((flat(rhs_s[:, mid, :]) + around) / (4.0 + flat(helm[...]))).reshape(lev, clat, LANES)
+    stores.append(pltpu.make_async_copy(pressure, pressure_o, out_sem.at[bands]))
+    stores[-1].start()
     for store in stores:
         store.wait()
 
@@ -317,7 +321,7 @@
             pltpu.SMEM(depth.shape, jnp.int32),
             *[pltpu.VMEM(t, F32) for t in (fields.shape, frac.shape, helm.shape, *tiles, fields.shape, frac.shape)],
             pltpu.SemaphoreType.DMA((4 + len(tiles),)),
-            pltpu.SemaphoreType.DMA((2 * lev,)),
+            pltpu.SemaphoreType.DMA((clat // BAND + 1,)),
         ],
         compiler_params=pltpu.CompilerParams(vmem_limit_bytes=60 << 20),
         name="update",

time: 17.9 us -> 17 us (0.950)
  Pallas kernels: 17.1 us -> 16.2 us
    pallas_call x1, Pallas kernels: 4.48 us -> 3.63 us  [local(): pl.pallas_call(functools.partial(update, lev, clat), out_shape=[jax.Shape...]
where the time goes in v4:
time: 17 us; the launch traced here: 16.9 us
  Pallas kernels  16.2 us (95%)
  between operations  0.64 us (4%)
    pallas_call x1, Pallas kernels, local(): pl.pallas_call(functools.partial(exchange, lev, clat), out_shape=[jax.Sha...  12.6 us
    pallas_call x1, Pallas kernels, local(): pl.pallas_call(functools.partial(update, lev, clat), out_shape=[jax.Shape...  3.63 us

profile of v4, /device:TPU:0, one launch (start us, length us, event | category | flops | bytes accessed | tf_op | source)
XLA Modules:
  0.0 16.9 jit_solution(1428723592951001322)
XLA Ops:
  0.6 12.6 %exchange.1 = (f32[2,5,4,8,128]{4,3,2,1,0:T(8,128)}, f32[4,8,128]{2,1,0:T(8,128)}, f32[6,8,128]{2,1,0:T(8,128)}, f32[6,8,128]{2,1,0:T(8,128)}, f32[3,8,128]{2,1,...) custom-call(s32[32]{0:T(128)} %refs_0_.1, f32[5,4,32,128]{3,2,1,0:T(8,128)} %refs_1_.1, ...), custom_call_target="tpu_custom_call" | custom-call | tf_op jit(solution)/shard_map/exchange/pallas_call | solution.py:293
  13.2 3.6 %update.1 = (f32[5,4,32,128]{3,2,1,0:T(8,128)}, f32[4,32,128]{2,1,0:T(8,128)}) custom-call(s32[32]{0:T(128)} %refs_0_.1, f32[5,4,32,128]{3,2,1,0:T(8,128)} %refs_1_.1, f32[4,32,128]{2,1,0:T(8,128)} %refs_2_.1, f32[4,32,128]{2,1,0:T(8,128)} %refs_3_.1, f32[2,5,4,8,128]{4,3,2,1,0:T(8,128)} %get-tuple-element.10.refs_4_, ...), custom_call_target="tpu_custom_call" | custom-call | tf_op jit(solution)/shard_map/update/pallas_call | solution.py:310
